TPU v7x, 32 devices: a whole 2x2x4 slice. The times are simulated.
32 devices in a mesh: rows: 8 (over z, x), cols: 4 (over y, core).
Axes of the slice: x: 2, y: 2, z: 4, core: 2. Of those that a mesh axis runs over, the one named last changes fastest.
Arguments:
- ham_tiles: bfloat16 [32, 8, 256, 256], P('rows', 'cols'), may hold values from -0.0625 to 0.0625
- tile_cols: int32 [32, 8], P('rows'), may hold values from -4 to 35, as said below
- tile_count: int32 [32], P('rows'), may hold values from 1 to 8
- term_prev: bfloat16 [8192, 1024], P('rows', 'cols'), may hold values from -0.29882812 to 0.29882812
- term_now: bfloat16 [8192, 1024], P('rows', 'cols'), may hold values from -0.29882812 to 0.29882812
- density_prev: float32 [8192, 1024], P('rows', 'cols'), may hold values from -0.3 to 0.3
- cheb_coef: float32 [3], replicated, may hold values from -1.5 to 1.5
- atom_sizes: int32 [1024], replicated, may hold values from 1 to 16, 8192 in all
- pair_atoms: int32 [64, 2], P('cols'), may hold values from 0 to 1023
Outputs:
- density: float32 [8192, 1024], P('rows', 'cols')
- wiberg: float32 [64], P('cols')
Inputs may be any that keep to these rules, and one draw needn't show every extreme that they name: tile_cols[i, 0] = i; the other slots of row i are distinct column tiles within 4 of i, possibly outside 0 to 32 - 1 (then not live).
All inputs are finite; a program needn't handle non-finite values.
Results may differ from a plain program's by a relative error of at most 0.006.
Values may be sent and summed in bfloat16 or wider, within the bound.
A program may use at most 64 MiB of HBM per device.

v0:
```python
import jax
import jax.numpy as jnp
from jax import lax
from jax.sharding import PartitionSpec as P

MAXF = 16


def padded(block, sides, width):
    for axis, dim in sides:
        count = lax.axis_size(axis)
        forward = [(i, i + 1) for i in range(count - 1)]
        backward = [(target, source) for source, target in forward]
        low = lax.ppermute(
            lax.slice_in_dim(block, block.shape[dim] - width, None, axis=dim), axis, forward
        )
        high = lax.ppermute(lax.slice_in_dim(block, 0, width, axis=dim), axis, backward)
        block = jnp.concatenate([low, block, high], axis=dim)
    return block


def on_device(
    ham_tiles,
    tile_cols,
    tile_count,
    term_prev,
    term_now,
    density_prev,
    cheb_coef,
    atom_sizes,
    pair_atoms,
):
    nrows = lax.axis_size("rows")
    row_blocks = tile_count.shape[0]
    tile = ham_tiles.shape[2]
    slots = tile_cols.shape[1]
    local_width = term_now.shape[1]
    first_block = lax.axis_index("rows") * row_blocks
    local_rows = jnp.arange(row_blocks, dtype=jnp.int32)
    shifts = tile_cols - (first_block + local_rows)[:, None]
    slot_ids = jnp.arange(slots, dtype=jnp.int32)
    live = (
        (slot_ids[None, :] < tile_count[:, None])
        & (tile_cols >= 0)
        & (tile_cols < row_blocks * nrows)
    )
    position = jnp.clip(shifts + row_blocks + local_rows[:, None], 0, 3 * row_blocks - 1)
    live_mask = live[:, :, None, None].astype(jnp.bfloat16)

    def select(current):
        extended = padded(current, (("rows", 0),), row_blocks * tile)
        tiles = extended.reshape(3 * row_blocks, tile, local_width)
        return tiles[position]

    def apply_with(masked, current):
        chosen = select(current)
        product = jnp.einsum("lkab,lkbw->law", masked, chosen, preferred_element_type=jnp.float32)
        return product.reshape(row_blocks * tile, local_width)

    previous, current = (term_prev, term_now)
    density = density_prev
    masked_all = lax.all_gather(ham_tiles, "cols", axis=1, tiled=True) * live_mask
    first_product = apply_with(masked_all, current)
    for step in range(3):
        if step == 0:
            product = first_product
        else:
            product = apply_with(masked_all, current)
        nxt = (2.0 * product - previous.astype(jnp.float32)).astype(jnp.bfloat16)
        density = density + cheb_coef[step] * nxt.astype(jnp.float32)
        previous, current = (current, nxt)
    offsets = jnp.cumsum(atom_sizes) - atom_sizes
    first_atom = pair_atoms[:, 0]
    second_atom = pair_atoms[:, 1]
    start = offsets[first_atom]
    count_a = atom_sizes[first_atom]
    count_b = atom_sizes[second_atom]
    my_pairs = pair_atoms.shape[0]
    inner = jnp.arange(MAXF, dtype=jnp.int32)
    global_rows = first_block * tile + jnp.arange(row_blocks * tile, dtype=jnp.int32)
    row_keep = (global_rows[None, :] >= start[:, None]) & (
        global_rows[None, :] < (start + count_a)[:, None]
    )
    col_keep = (inner[None, :] < count_b[:, None]).astype(jnp.float32)
    squares = (density * density).reshape(row_blocks * tile, my_pairs, MAXF)
    by_pair = jnp.sum(squares * col_keep[None, :, :], axis=2)
    partial_sum = jnp.sum(jnp.where(row_keep.T, by_pair, 0.0), axis=0)
    wiberg = lax.psum(partial_sum, "rows")
    return (density, wiberg)


def solution(mesh):
    return jax.shard_map(
        on_device,
        mesh=mesh,
        in_specs=(
            P("rows", "cols", None, None),
            P("rows", None),
            P("rows"),
            P("rows", "cols"),
            P("rows", "cols"),
            P("rows", "cols"),
            P(),
            P(),
            P("cols", None),
        ),
        out_specs=(P("rows", "cols"), P("cols")),
        check_vma=False,
    )
```

profile of v0, /device:TPU:0, one launch (start us, length us, event | category | flops | bytes accessed | tf_op | source)
XLA Modules:
  0.0 155.1 jit_solution(16937124953616179820)
XLA Ops:
  7.2 0.7 all-gather.2.cloned.1.call-update
  7.9 4.9 %collective-permute-start = (bf16[1024,256]{1,0:T(8,128)(2,1)}, bf16[1024,256]{1,0:T(8,128)(2,1)S(1)}, u32[]{:S(2)}, u32[]{:S(2)}) collective-permute-start(bf16[1024,256]{1,0:T(8,128)(2,1)} %param.13), channel_id=1, source_target_pairs={{0,4},{4,8},{8,12},{12,16},{16,20},{20,24},{24,28},{1,5},{5,9},{9,... | collective-permute-start | bytes 1572872 | tf_op jit(solution)/shard_map/ppermute | solution.py:14
  12.8 1.3 collective-permute-start.1
  14.1 0.8 compare_select_fusion
  14.9 1.0 reduce-window.9
  16.0 0.8 fusion.36
  16.8 18.7 %collective-permute-done = bf16[1024,256]{1,0:T(8,128)(2,1)S(1)} collective-permute-done((bf16[1024,256]{1,0:T(8,128)(2,1)}, bf16[1024,256]{1,0:T(8,128)(2,1)S(1)}, u32[]{:S(2)}, u32[]{:S(2)}) %collective-permute-start) | collective-permute-done | bytes 524320 | tf_op jit(solution)/shard_map/ppermute | solution.py:14
  35.5 1.1 pad_maximum_fusion
  36.6 2.8 %gather_fusion = bf16[32,256,256]{2,1,0:T(8,128)(2,1)} fusion(bf16[12,256,256]{2,1,0:T(8,128)(2,1)S(1)} %bitcast.51, s32[1024]{0:T(1024)S(1)} %pad_clamp_fusion.2), kind=kCustom, calls=%fused_computation | custom fusion | bytes 8388736 | tf_op jit(solution)/shard_map/gather | solution.py:53
  39.4 7.4 %all-gather.2.cloned.1.call-done = bf16[4,8,256,256]{3,2,1,0:T(8,128)(2,1)} async-done(((bf16[4,2,256,256]{3,2,1,0:T(8,128)(2,1)}), bf16[4,8,256,256]{3,2,1,0:T(8,128)(2,1)}) %all-gather.2.cloned.1.call-update) | async-done | bytes 4194320 | tf_op jit(solution)/shard_map/all_gather | solution.py:62
  46.8 4.8 %fusion.24 = f32[4,256,256]{2,1,0:T(8,128)S(1)} fusion(bf16[4,8,256,256]{3,2,1,0:T(8,128)(2,1)} %bitcast.53, bf16[4,8,256,256]{3,2,1,0:T(8,128)(2,1)} %all-gather.2.cloned.1.call-done, bf16[4,8]{1,0:T(4,128)(2,1)S(1)} %fusion.36), kind=kOutput, calls=%fused_computation.23 | convolution fusion | flops 1076101120 | bytes 9437248 | tf_op jit(solution)/shard_map/lkab,lkbw->law/dot_general | solution.py:57
  51.6 0.1 fusion.32
  51.7 3.4 %collective-permute-start.2 = (bf16[1024,256]{1,0:T(8,128)(2,1)S(1)}, bf16[1024,256]{1,0:T(8,128)(2,1)S(1)}, u32[]{:S(2)}, u32[]{:S(2)}) collective-permute-start(bf16[1024,256]{1,0:T(8,128)(2,1)S(1)} %fusion.32), channel_id=1, source_target_pairs={{0,4},{4,8},{8,12},{12,16},{16,20},{20,24},{24,28},{1,5},{5,9},{9,... | collective-permute-start | bytes 1572872 | tf_op jit(solution)/shard_map/ppermute | solution.py:14
  55.2 1.3 collective-permute-start.3
  56.7 21.3 %collective-permute-done.2 = bf16[1024,256]{1,0:T(8,128)(2,1)S(1)} collective-permute-done((bf16[1024,256]{1,0:T(8,128)(2,1)S(1)}, bf16[1024,256]{1,0:T(8,128)(2,1)S(1)}, u32[]{:S(2)}, u32[]{:S(2)}) %collective-permute-start.2) | collective-permute-done | bytes 524320 | tf_op jit(solution)/shard_map/ppermute | solution.py:14
  78.0 2.8 %gather_fusion.1 = bf16[32,256,256]{2,1,0:T(8,128)(2,1)} fusion(bf16[12,256,256]{2,1,0:T(8,128)(2,1)S(1)} %bitcast.52, s32[1024]{0:T(1024)S(1)} %pad_clamp_fusion.2), kind=kCustom, calls=%fused_computation.1 | custom fusion | bytes 8388736 | tf_op jit(solution)/shard_map/gather | solution.py:53
  80.8 4.8 %fusion.21 = f32[4,256,256]{2,1,0:T(8,128)S(1)} fusion(bf16[4,8,256,256]{3,2,1,0:T(8,128)(2,1)} %bitcast.55, bf16[4,8,256,256]{3,2,1,0:T(8,128)(2,1)} %all-gather.2.cloned.1.call-done, bf16[4,8]{1,0:T(4,128)(2,1)S(1)} %fusion.36), kind=kOutput, calls=%fused_computation.22 | convolution fusion | flops 1076101120 | bytes 9437248 | tf_op jit(solution)/shard_map/lkab,lkbw->law/dot_general | solution.py:57
  85.8 4.4 %collective-permute-start.4 = (bf16[1024,256]{1,0:T(8,128)(2,1)S(1)}, bf16[1024,256]{1,0:T(8,128)(2,1)S(1)}, u32[]{:S(2)}, u32[]{:S(2)}) collective-permute-start(bf16[1024,256]{1,0:T(8,128)(2,1)S(1)} %fusion.31), channel_id=1, source_target_pairs={{0,4},{4,8},{8,12},{12,16},{16,20},{20,24},{24,28},{1,5},{5,9},{9,... | collective-permute-start | bytes 1572872 | tf_op jit(solution)/shard_map/ppermute | solution.py:14
  90.2 1.3 collective-permute-start.5
  91.5 0.6 gather_fusion.5
  92.2 0.6 gather_fusion.4
  92.8 0.6 gather_fusion.3
  93.5 0.6 fusion.41
  94.2 18.0 %collective-permute-done.4 = bf16[1024,256]{1,0:T(8,128)(2,1)S(1)} collective-permute-done((bf16[1024,256]{1,0:T(8,128)(2,1)S(1)}, bf16[1024,256]{1,0:T(8,128)(2,1)S(1)}, u32[]{:S(2)}, u32[]{:S(2)}) %collective-permute-start.4) | collective-permute-done | bytes 524320 | tf_op jit(solution)/shard_map/ppermute | solution.py:14
  112.2 1.1 pad_maximum_fusion.2
  113.3 2.8 %gather_fusion.2 = bf16[32,256,256]{2,1,0:T(8,128)(2,1)} fusion(bf16[12,256,256]{2,1,0:T(8,128)(2,1)S(1)} %bitcast.50, s32[1024]{0:T(1024)S(1)} %pad_clamp_fusion.2), kind=kCustom, calls=%fused_computation.2 | custom fusion | bytes 8388736 | tf_op jit(solution)/shard_map/gather | solution.py:53
  116.1 4.8 %fusion.18 = f32[4,256,256]{2,1,0:T(8,128)S(1)} fusion(bf16[4,8,256,256]{3,2,1,0:T(8,128)(2,1)} %bitcast.54, bf16[4,8,256,256]{3,2,1,0:T(8,128)(2,1)} %all-gather.2.cloned.1.call-done, bf16[4,8]{1,0:T(4,128)(2,1)S(1)} %fusion.36), kind=kOutput, calls=%fused_computation.21 | convolution fusion | flops 1076101120 | bytes 9437248 | tf_op jit(solution)/shard_map/lkab,lkbw->law/dot_general | solution.py:57
  121.0 3.2 %fusion.39 = (f32[1024,256]{1,0:T(8,128)S(1)}, f32[1024,256]{1,0:T(8,128)}) fusion(f32[4,256,256]{2,1,0:T(8,128)S(1)} %fusion.18, f32[]{:T(128)} %bitcast.12, bf16[1024,256]{1,0:T(8,128)(2,1)S(1)} %fusion.31, f32[]{:T(128)} %bitcast.6, f32[1024,256]{1,0:T(8,128)S(1)} %copy-done.2, bf16[1024,256]{1,0:T(8,128)(2,1)S(1)} %fusion.32, f32[]{:T(128)} %bitcast), kind=kLoop, calls=%fused_computation.54 | loop fusion | flops 3145728 | bytes 5242892 | tf_op jit(solution)/shard_map/mul | solution.py:85
  124.1 0.3 copy.21
  124.5 0.3 multiply_reduce_fusion
  124.8 0.2 select_reduce_fusion
  124.9 23.3 %psum.7 = f32[16]{0:T(128)} all-reduce(f32[16]{0:T(128)S(1)} %select_reduce_fusion), channel_id=1, replica_groups=mesh['rows'=8,'cols'=4] {'rows'}, use_global_device_ids=true, to_apply=%region_4.5 | all-reduce | flops 16 | bytes 128 | tf_op jit(solution)/shard_map/psum | solution.py:88
  (30 shorter events, 0.8 us)
Async XLA Ops:
  7.2 39.6 %all-gather.2.cloned.1.call-start = ((), (), s32[]{:S(2)}) async-start(), calls=%async_computation | async-start | bytes 5242880 | tf_op jit(solution)/shard_map/all_gather | solution.py:62
  7.9 27.6 %collective-permute-start = (bf16[1024,256]{1,0:T(8,128)(2,1)}, bf16[1024,256]{1,0:T(8,128)(2,1)S(1)}, u32[]{:S(2)}, u32[]{:S(2)}) collective-permute-start(bf16[1024,256]{1,0:T(8,128)(2,1)} %param.13), channel_id=1, source_target_pairs={{0,4},{4,8},{8,12},{12,16},{16,20},{20,24},{24,28},{1,5},{5,9},{9,... | collective-permute-start | bytes 1572872 | tf_op jit(solution)/shard_map/ppermute | solution.py:14
  12.8 22.7 %collective-permute-start.1 = (bf16[1024,256]{1,0:T(8,128)(2,1)}, bf16[1024,256]{1,0:T(8,128)(2,1)S(1)}, u32[]{:S(2)}, u32[]{:S(2)}) collective-permute-start(bf16[1024,256]{1,0:T(8,128)(2,1)} %param.13), channel_id=1, source_target_pairs={{4,0},{8,4},{12,8},{16,12},{20,16},{24,20},{28,24},{5,1},{9,5},{13... | collective-permute-start | bytes 1572872 | tf_op jit(solution)/shard_map/ppermute | solution.py:17
  46.8 4.8 %copy-start.3 = (bf16[1024,256]{1,0:T(8,128)(2,1)S(1)}, bf16[1024,256]{1,0:T(8,128)(2,1)}, u32[]{:S(2)}) copy-start(bf16[1024,256]{1,0:T(8,128)(2,1)} %param.12) | copy-start | bytes 1572868
  46.8 9.8 %copy-start.5 = (s32[16,2]{0,1:T(2,128)S(1)}, s32[16,2]{0,1:T(2,128)}, u32[]{:S(2)}) copy-start(s32[16,2]{0,1:T(2,128)} %param.17) | copy-start | bytes 388
  46.8 9.8 %copy-start = (s32[1024]{0:T(1024)S(1)}, s32[1024]{0:T(1024)}, u32[]{:S(2)}) copy-start(s32[1024]{0:T(1024)} %param.16) | copy-start | bytes 12292
  51.7 26.2 %collective-permute-start.2 = (bf16[1024,256]{1,0:T(8,128)(2,1)S(1)}, bf16[1024,256]{1,0:T(8,128)(2,1)S(1)}, u32[]{:S(2)}, u32[]{:S(2)}) collective-permute-start(bf16[1024,256]{1,0:T(8,128)(2,1)S(1)} %fusion.32), channel_id=1, source_target_pairs={{0,4},{4,8},{8,12},{12,16},{16,20},{20,24},{24,28},{1,5},{5,9},{9,... | collective-permute-start | bytes 1572872 | tf_op jit(solution)/shard_map/ppermute | solution.py:14
  55.2 22.8 %collective-permute-start.3 = (bf16[1024,256]{1,0:T(8,128)(2,1)S(1)}, bf16[1024,256]{1,0:T(8,128)(2,1)S(1)}, u32[]{:S(2)}, u32[]{:S(2)}) collective-permute-start(bf16[1024,256]{1,0:T(8,128)(2,1)S(1)} %fusion.32), channel_id=1, source_target_pairs={{4,0},{8,4},{12,8},{16,12},{20,16},{24,20},{28,24},{5,1},{9,5},{13... | collective-permute-start | bytes 1572872 | tf_op jit(solution)/shard_map/ppermute | solution.py:17
  80.8 4.8 %copy-start.1 = (bf16[1024,256]{1,0:T(8,128)(2,1)S(1)}, bf16[1024,256]{1,0:T(8,128)(2,1)}, u32[]{:S(2)}) copy-start(bf16[1024,256]{1,0:T(8,128)(2,1)} %param.13) | copy-start | bytes 1572868
  80.8 12.7 %copy-start.4 = (f32[3]{0:T(128)S(1)}, f32[3]{0:T(128)}, u32[]{:S(2)}) copy-start(f32[3]{0:T(128)} %param.15) | copy-start | bytes 40
  85.8 26.4 %collective-permute-start.4 = (bf16[1024,256]{1,0:T(8,128)(2,1)S(1)}, bf16[1024,256]{1,0:T(8,128)(2,1)S(1)}, u32[]{:S(2)}, u32[]{:S(2)}) collective-permute-start(bf16[1024,256]{1,0:T(8,128)(2,1)S(1)} %fusion.31), channel_id=1, source_target_pairs={{0,4},{4,8},{8,12},{12,16},{16,20},{20,24},{24,28},{1,5},{5,9},{9,... | collective-permute-start | bytes 1572872 | tf_op jit(solution)/shard_map/ppermute | solution.py:14
  90.2 22.0 %collective-permute-start.5 = (bf16[1024,256]{1,0:T(8,128)(2,1)S(1)}, bf16[1024,256]{1,0:T(8,128)(2,1)}, u32[]{:S(2)}, u32[]{:S(2)}) collective-permute-start(bf16[1024,256]{1,0:T(8,128)(2,1)S(1)} %fusion.31), channel_id=1, source_target_pairs={{4,0},{8,4},{12,8},{16,12},{20,16},{24,20},{28,24},{5,1},{9,5},{13... | collective-permute-start | bytes 1572872 | tf_op jit(solution)/shard_map/ppermute | solution.py:17
  116.1 4.8 %copy-start.2 = (f32[1024,256]{1,0:T(8,128)S(1)}, f32[1024,256]{1,0:T(8,128)}, u32[]{:S(2)}) copy-start(f32[1024,256]{1,0:T(8,128)} %param.14) | copy-start | bytes 3145732
Sparse Core Ops, SparseCore 0:
  9.6 37.1 all-gather.1
where the time goes:
time: 156 us; the launch traced here: 155 us
  waiting for transfers between devices  66 us (42%)
  blocking collectives  23.3 us (15%)
  starting transfers between devices  16.6 us (11%)
  matrix products  14.4 us (9%)
  between operations  14.2 us (9%)
  local copies, waits for them, and re-layouts  11.5 us (7%)
  other arithmetic  9 us (6%)
    ppermute x3, waiting for transfers between devices, padded(): lax.ppermute(lax.slice_in_dim(block, block.shape[dim] - width, None, axis...  58 us
    psum x1, blocking collectives, on_device(): wiberg = lax.psum(partial_sum, 'rows')  23.3 us
    dot_general x3, matrix products, apply_with(): jnp.einsum('lkab,lkbw->law', masked, chosen, preferred_element_type=jnp.f...  14.4 us
    ppermute x3, starting transfers between devices, padded(): lax.ppermute(lax.slice_in_dim(block, block.shape[dim] - width, None, axis...  12.7 us
    gather x3, local copies, waits for them, and re-layouts, select(): return tiles[position]  8.33 us
    all_gather x1, waiting for transfers between devices, on_device(): lax.all_gather(ham_tiles, 'cols', axis=1, tiled=True) * live_mask  7.38 us
    ppermute x3, starting transfers between devices, padded(): lax.ppermute(lax.slice_in_dim(block, 0, width, axis=dim), axis, backward)  3.88 us
    mul x1, other arithmetic, on_device(): squares = (density * density).reshape(row_blocks * tile, my_pairs, MAXF)  3.19 us
  transfers between devices with their start and end apart: 7, of which 4 were waited for; matrix products, arithmetic and copies ran while one was open for 6% of the time, Pallas kernels for 0%

commit v1 on v0

v1 whole, which is shorter than its diff:
```python
import functools

import jax
import jax.numpy as jnp
from jax import lax
from jax.experimental import pallas as pl
from jax.experimental.pallas import tpu as pltpu
from jax.sharding import PartitionSpec as P

MAXF = 16
STEPS = 3
CHUNKS = 2
MESH = pl.DeviceIdType.MESH


def kernel(
    n,
    ham,
    cols_ref,
    count_ref,
    prev_ref,
    now_ref,
    dens_in,
    coef,
    sizes,
    pairs,
    dens,
    wib,
    hb,
    part,
    wbuf,
    h_send,
    h_recv,
    t_send,
    t_recv,
    w_send,
    w_recv,
    *bufs,
):
    ext = [bufs[t * CHUNKS : (t + 1) * CHUNKS] for t in range(STEPS)]
    me = lax.axis_index("rows")
    mc = lax.axis_index("cols")
    blocks, own_slots, tile, _ = ham.shape
    width = now_ref.shape[1] // CHUNKS
    zero_tile = 3 * blocks
    sib = mc + 1 - 2 * (mc % 2)
    far = (mc + 2) % 4

    barrier = pltpu.get_barrier_semaphore()

    def greet(j, carry):
        pl.semaphore_signal(barrier, inc=1, device_id={"rows": (me + j) % n}, device_id_type=MESH)
        return carry

    lax.fori_loop(1, n, greet, 0)
    pl.semaphore_signal(barrier, inc=1, device_id={"cols": sib}, device_id_type=MESH)
    pl.semaphore_signal(barrier, inc=1, device_id={"cols": far}, device_id_type=MESH)

    def put(t, ch, l, value):
        ext[t][ch][blocks + l] = value

    for ch in range(CHUNKS):
        for l in range(blocks):
            put(0, ch, l, now_ref[l * tile : (l + 1) * tile, ch * width : (ch + 1) * width])
    for t in range(STEPS):
        for ch in range(CHUNKS):
            ext[t][ch][zero_tile] = jnp.zeros((tile, width), jnp.bfloat16)
    pl.semaphore_wait(barrier, n + 1)

    def halo(t, ch, up):
        return pltpu.make_async_remote_copy(
            src_ref=ext[t][ch].at[pl.ds(blocks, blocks)],
            dst_ref=ext[t][ch].at[pl.ds(0 if up else 2 * blocks, blocks)],
            send_sem=t_send.at[t, ch, int(up)],
            recv_sem=t_recv.at[t, ch, int(up)],
            device_id={"rows": me + 1 if up else me - 1},
            device_id_type=MESH,
        )

    def send_halo(t, ch):
        @pl.when(me < n - 1)
        def _():
            halo(t, ch, True).start()

        @pl.when(me > 0)
        def _():
            halo(t, ch, False).start()

    def recv_halo(t, ch):
        @pl.when(me > 0)
        def _():
            halo(t, ch, True).wait_recv()

        @pl.when(me < n - 1)
        def _():
            halo(t, ch, False).wait_recv()

    def drain_halo(t, ch):
        @pl.when(me < n - 1)
        def _():
            halo(t, ch, True).wait_send()

        @pl.when(me > 0)
        def _():
            halo(t, ch, False).wait_send()

    def tiles(q, l):
        return pltpu.make_async_remote_copy(
            src_ref=hb.at[1, l] if q == 2 else ham.at[l],
            dst_ref=hb.at[q, l],
            send_sem=h_send.at[q, l],
            recv_sem=h_recv.at[q, l],
            device_id={"cols": far if q == 1 else sib},
            device_id_type=MESH,
        )

    for ch in range(CHUNKS):
        send_halo(0, ch)
        for l in range(blocks):
            if l % CHUNKS == ch:
                tiles(1, l).start()
    for l in range(blocks):
        tiles(0, l).start()

    dens[...] = dens_in[...]

    npairs = pairs.shape[0]
    natoms = sizes.shape[1]
    atom = lax.broadcasted_iota(jnp.int32, (npairs, natoms), 1)
    size_f = jnp.broadcast_to(sizes[...].astype(jnp.float32), (npairs, natoms))
    first = jnp.broadcast_to(pairs[:, 0:1], (npairs, natoms))
    second = jnp.broadcast_to(pairs[:, 1:2], (npairs, natoms))
    start = jnp.sum(jnp.where(atom < first, size_f, 0.0), axis=1, keepdims=True)
    count_a = jnp.sum(jnp.where(atom == first, size_f, 0.0), axis=1, keepdims=True)
    count_b = jnp.sum(jnp.where(atom == second, size_f, 0.0), axis=1, keepdims=True)
    all_cols = npairs * MAXF
    column = lax.broadcasted_iota(jnp.int32, (npairs, all_cols), 1)
    pair_id = lax.broadcasted_iota(jnp.int32, (npairs, all_cols), 0)
    inner = column - pair_id * MAXF
    mine = (inner >= 0) & (inner < MAXF)
    kept = mine & (inner.astype(jnp.float32) < jnp.broadcast_to(count_b, (npairs, all_cols)))

    def spread(value, where):
        return jnp.sum(
            jnp.where(where, jnp.broadcast_to(value, (npairs, all_cols)), 0.0), axis=0, keepdims=True
        )

    low = spread(start, mine)
    high = low + spread(count_a, kept)
    part[...] = jnp.zeros_like(part)

    for l in range(blocks):
        tiles(1, l).wait_recv()
        tiles(2, l).start()
    for q in (0, 2):
        for l in range(blocks):
            tiles(q, l).wait_recv()

    owners = (mc, sib, far, (sib + 2) % 4)
    base = me * blocks

    def where_is(l, slot):
        col = cols_ref[l, slot]
        live = (slot < count_ref[l]) & (col >= 0) & (col < blocks * n)
        return jnp.where(live, jnp.clip(col - base + blocks, 0, 3 * blocks - 1), zero_tile)

    for t in range(STEPS):
        for ch in range(CHUNKS):
            span = slice(ch * width, (ch + 1) * width)
            recv_halo(t, ch)

            def row(l, carry, t=t, ch=ch, span=span):
                acc = jnp.zeros((tile, width), jnp.float32)
                for q, owner in enumerate(owners):
                    for s in range(own_slots):
                        h = ham[l, s] if q == 0 else hb[q - 1, l, s]
                        v = ext[t][ch][where_is(l, owner * own_slots + s)]
                        acc += jnp.dot(h, v, preferred_element_type=jnp.float32)
                rows = pl.ds(pl.multiple_of(l * tile, tile), tile)
                if t == 0:
                    prev = prev_ref[rows, span]
                else:
                    prev = ext[t - 1][ch][blocks + l]
                nxt = (2.0 * acc - prev.astype(jnp.float32)).astype(jnp.bfloat16)
                value = dens[rows, span] + coef[t] * nxt.astype(jnp.float32)
                dens[rows, span] = value
                if t < STEPS - 1:
                    ext[t + 1][ch][blocks + l] = nxt
                else:
                    r = lax.broadcasted_iota(jnp.int32, (tile, width), 0) + (base + l) * tile
                    r = r.astype(jnp.float32)
                    keep = (r >= low[:, span]) & (r < high[:, span])
                    sq = jnp.where(keep, value * value, 0.0)
                    part[:, span] += jnp.sum(sq.reshape(tile // 8, 8, width), axis=0)
                return carry

            lax.fori_loop(0, blocks, row, 0)
            if t < STEPS - 1:
                send_halo(t + 1, ch)

    def share(j):
        return pltpu.make_async_remote_copy(
            src_ref=part,
            dst_ref=wbuf.at[me],
            send_sem=w_send.at[j],
            recv_sem=w_recv.at[me],
            device_id={"rows": (me + j) % n},
            device_id_type=MESH,
        )

    def landed(j):
        source = (me + j) % n
        return pltpu.make_async_remote_copy(
            src_ref=part,
            dst_ref=wbuf.at[source],
            send_sem=w_send.at[j],
            recv_sem=w_recv.at[source],
            device_id={"rows": source},
            device_id_type=MESH,
        )

    def push(j, carry):
        share(j).start()
        return carry

    lax.fori_loop(1, n, push, 0)
    for l in range(blocks):
        for q in range(3):
            tiles(q, l).wait_send()
    for t in range(STEPS):
        for ch in range(CHUNKS):
            drain_halo(t, ch)

    def collect(j, total):
        landed(j).wait_recv()
        return total + wbuf[(me + j) % n]

    total = lax.fori_loop(1, n, collect, part[...])
    summed = jnp.broadcast_to(jnp.sum(total, axis=0, keepdims=True), (npairs, all_cols))
    wib[...] = jnp.sum(jnp.where(mine, summed, 0.0), axis=1, keepdims=True)

    def drain(j, carry):
        share(j).wait_send()
        return carry

    lax.fori_loop(1, n, drain, 0)


def on_device(n, ham, cols, count, prev, now, dens_prev, coef, sizes, pairs):
    blocks, own_slots, tile, _ = ham.shape
    rows, width = now.shape
    npairs = pairs.shape[0]
    vmem = pl.BlockSpec(memory_space=pltpu.VMEM)
    smem = pl.BlockSpec(memory_space=pltpu.SMEM)
    dma = pltpu.SemaphoreType.DMA
    dens, wib = pl.pallas_call(
        functools.partial(kernel, n),
        out_shape=(
            jax.ShapeDtypeStruct((rows, width), jnp.float32),
            jax.ShapeDtypeStruct((npairs, 1), jnp.float32),
        ),
        in_specs=[vmem, smem, smem, vmem, vmem, vmem, smem, vmem, vmem],
        out_specs=(vmem, vmem),
        scratch_shapes=[
            pltpu.VMEM((3, blocks, own_slots, tile, tile), jnp.bfloat16),
            pltpu.VMEM((8, width), jnp.float32),
            pltpu.VMEM((n, 8, width), jnp.float32),
            dma((3, blocks)),
            dma((3, blocks)),
            dma((STEPS, CHUNKS, 2)),
            dma((STEPS, CHUNKS, 2)),
            dma((n,)),
            dma((n,)),
        ]
        + [pltpu.VMEM((3 * blocks + 1, tile, width // CHUNKS), jnp.bfloat16)] * (STEPS * CHUNKS),
        compiler_params=pltpu.CompilerParams(
            collective_id=0, has_side_effects=True, vmem_limit_bytes=48 << 20
        ),
    )(ham, cols, count, prev, now, dens_prev, coef, sizes.reshape(1, -1), pairs)
    return dens, wib.reshape(npairs)


def solution(mesh):
    return jax.shard_map(
        functools.partial(on_device, mesh.shape["rows"]),
        mesh=mesh,
        in_specs=(
            P("rows", "cols", None, None),
            P("rows", None),
            P("rows"),
            P("rows", "cols"),
            P("rows", "cols"),
            P("rows", "cols"),
            P(),
            P(),
            P("cols", None),
        ),
        out_specs=(P("rows", "cols"), P("cols")),
        check_vma=False,
    )
```

time: 156 us -> 94.8 us (0.61)
  Pallas kernels: 0 us -> 86.3 us
  waiting for transfers between devices: 66 us -> 0 us
  blocking collectives: 23.3 us -> 0 us
  starting transfers between devices: 16.6 us -> 0 us
  matrix products: 14.4 us -> 0 us
  between operations: 14.2 us -> 0.66 us
  other arithmetic: 9 us -> 0.63 us
  local copies, waits for them, and re-layouts: 11.5 us -> 6.87 us
    pallas_call x0 -> x1, Pallas kernels: none -> 86.3 us  [on_device(): pl.pallas_call(functools.partial(kernel, n), out_shape=(jax.ShapeDtypeStr...]
    ppermute x6 -> x0, waiting for transfers between devices: 58 us -> none  [the longest x3 58 us: padded(): lax.ppermute(lax.slice_in_dim(block, block.shape[dim] - width, None, axis...]
    psum x1 -> x0, blocking collectives: 23.3 us -> none  [on_device(): wiberg = lax.psum(partial_sum, 'rows')]
    ppermute x6 -> x0, starting transfers between devices: 16.6 us -> none  [the longest x3 12.7 us: padded(): lax.ppermute(lax.slice_in_dim(block, block.shape[dim] - width, None, axis...]
    dot_general x3 -> x0, matrix products: 14.4 us -> none  [apply_with(): jnp.einsum('lkab,lkbw->law', masked, chosen, preferred_element_type=jnp.f...]
    gather x6 -> x0, local copies, waits for them, and re-layouts: 10.3 us -> none  [the longest x3 8.33 us: select(): return tiles[position]]
    all_gather x1 -> x0, waiting for transfers between devices: 7.38 us -> none  [on_device(): lax.all_gather(ham_tiles, 'cols', axis=1, tiled=True) * live_mask]
    unnamed x12 -> x20, local copies, waits for them, and re-layouts: 0.02 us -> 6.87 us
  transfers between devices with their start and end apart: 7 -> 0, of which waited for: 4 -> 0; matrix products, arithmetic and copies ran while one was open for 6% -> 0% of each run, Pallas kernels for 0% -> 0%
where the time goes in v1:
time: 94.8 us; the launch traced here: 94.5 us
  Pallas kernels  86.3 us (91%)
  local copies, waits for them, and re-layouts  6.87 us (7%)
    pallas_call x1, Pallas kernels, on_device(): pl.pallas_call(functools.partial(kernel, n), out_shape=(jax.ShapeDtypeStr...  86.3 us
    unnamed x20, local copies, waits for them, and re-layouts  6.87 us

profile of v1, /device:TPU:0, one launch (start us, length us, event | category | flops | bytes accessed | tf_op | source)
XLA Modules:
  0.0 94.5 jit_solution(8855256637681629910)
XLA Ops:
  0.6 0.0 copy-start.8
  0.6 0.7 copy-done.8
  1.3 0.0 copy-start.4
  1.3 0.0 copy-start.5
  1.3 0.0 copy-start.6
  1.3 0.0 copy-start.7
  1.3 0.1 copy.12.pairs
  1.4 0.6 copy-done.4
  2.0 0.0 copy-done.5
  2.0 0.0 copy-done.6
  2.0 0.0 copy-done.7
  2.0 0.0 copy-start
  2.0 1.2 %copy-done = bf16[4,2,256,256]{3,2,1,0:T(8,128)(2,1)S(1)} copy-done((bf16[4,2,256,256]{3,2,1,0:T(8,128)(2,1)S(1)}, bf16[4,2,256,256]{3,2,1,0:T(8,128)(2,1)}, u32[]{:S(2)}) %copy-start) | copy-done | bytes 1048600
  3.2 0.0 copy-start.1
  3.2 1.2 %copy-done.1 = f32[1024,256]{1,0:T(8,128)S(1)} copy-done((f32[1024,256]{1,0:T(8,128)S(1)}, f32[1024,256]{1,0:T(8,128)}, u32[]{:S(2)}) %copy-start.1) | copy-done | bytes 1048600
  4.5 0.0 copy-start.2
  4.5 1.0 %copy-done.2 = bf16[1024,256]{1,0:T(8,128)(2,1)S(1)} copy-done((bf16[1024,256]{1,0:T(8,128)(2,1)S(1)}, bf16[1024,256]{1,0:T(8,128)(2,1)}, u32[]{:S(2)}) %copy-start.2) | copy-done | bytes 524312
  5.5 0.0 copy-start.3
  5.5 1.0 %copy-done.3 = bf16[1024,256]{1,0:T(8,128)(2,1)S(1)} copy-done((bf16[1024,256]{1,0:T(8,128)(2,1)S(1)}, bf16[1024,256]{1,0:T(8,128)(2,1)}, u32[]{:S(2)}) %copy-start.3) | copy-done | bytes 524312
  6.6 86.3 %shard_map.104 = (f32[1024,256]{1,0:T(8,128)S(1)}, f32[16,1]{1,0:T(8,128)S(1)}) custom-call(bf16[4,2,256,256]{3,2,1,0:T(8,128)(2,1)S(1)} %copy-done, s32[4,8]{1,0:T(4,128)S(1)} %copy-done.5, s32[4]{0:T(128)S(1)} %copy-done.6, bf16[1024,256]{1,0:T(8,128)(2,1)S(1)} %copy-done.2, bf16[1024,256]{1,0:T(8,128)(2,1)S(1)} %copy-done.3, f32[1024,256]{1,0:T(8,128)S(1)} %copy-done.1, ...), custom_call_target="tpu_custom_call" | custom-call | tf_op jit(solution)/shard_map/pallas_call | solution.py:256
  92.9 0.6 reduce
  93.5 1.0 %copy.14 = f32[1024,256]{1,0:T(8,128)} copy(f32[1024,256]{1,0:T(8,128)S(1)} %get-tuple-element.8) | data formatting | bytes 2097152
Async XLA Ops:
  0.6 0.7 copy-start.8
  1.3 0.7 copy-start.4
  1.3 0.7 copy-start.5
  1.3 0.7 copy-start.6
  1.3 0.7 copy-start.7
  2.0 1.2 %copy-start = (bf16[4,2,256,256]{3,2,1,0:T(8,128)(2,1)S(1)}, bf16[4,2,256,256]{3,2,1,0:T(8,128)(2,1)}, u32[]{:S(2)}) copy-start(bf16[4,2,256,256]{3,2,1,0:T(8,128)(2,1)} %ham.1) | copy-start | bytes 3145732
  3.2 1.2 %copy-start.1 = (f32[1024,256]{1,0:T(8,128)S(1)}, f32[1024,256]{1,0:T(8,128)}, u32[]{:S(2)}) copy-start(f32[1024,256]{1,0:T(8,128)} %dens_in.1) | copy-start | bytes 3145732
  4.5 1.0 %copy-start.2 = (bf16[1024,256]{1,0:T(8,128)(2,1)S(1)}, bf16[1024,256]{1,0:T(8,128)(2,1)}, u32[]{:S(2)}) copy-start(bf16[1024,256]{1,0:T(8,128)(2,1)} %prev_ref.1) | copy-start | bytes 1572868
  5.5 1.0 %copy-start.3 = (bf16[1024,256]{1,0:T(8,128)(2,1)S(1)}, bf16[1024,256]{1,0:T(8,128)(2,1)}, u32[]{:S(2)}) copy-start(bf16[1024,256]{1,0:T(8,128)(2,1)} %now_ref.1) | copy-start | bytes 1572868

commit v2 on v1

v2 whole, which is shorter than its diff:
```python
import functools

import jax
import jax.numpy as jnp
from jax import lax
from jax.experimental import pallas as pl
from jax.experimental.pallas import tpu as pltpu
from jax.sharding import PartitionSpec as P

MAXF = 16
STEPS = 3
MESH = pl.DeviceIdType.MESH


def kernel(
    n,
    ham,
    cols_ref,
    count_ref,
    prev_ref,
    now_ref,
    dens_in,
    coef,
    sizes,
    pairs,
    dens,
    wib,
    hown,
    hb,
    pv,
    fin,
    vmine,
    vpair,
    smine,
    spair,
    part,
    bounds,
    wbuf,
    h_send,
    h_recv,
    t_send,
    t_recv,
    i_send,
    i_recv,
    r_send,
    r_recv,
    w_send,
    w_recv,
    l_sem,
    *bufs,
):
    ext, ret = bufs[:STEPS], bufs[STEPS:]
    me = lax.axis_index("rows")
    mc = lax.axis_index("cols")
    x = me % 2
    y = 1 - x
    mate = me + 1 - 2 * x
    blocks, own_slots, tile, _ = ham.shape
    half = now_ref.shape[1] // 2
    zero_tile = 4 * blocks
    sib = mc + 1 - 2 * (mc % 2)
    far = (mc + 2) % 4
    here = pl.ds(pl.multiple_of(x * half, half), half)
    there = pl.ds(pl.multiple_of(y * half, half), half)

    def remote(src, dst, send, recv, device):
        return pltpu.make_async_remote_copy(
            src_ref=src, dst_ref=dst, send_sem=send, recv_sem=recv, device_id=device, device_id_type=MESH
        )

    local = [pltpu.make_async_copy(ham, hown, l_sem.at[0]), pltpu.make_async_copy(dens_in, dens, l_sem.at[1])]
    for l in range(blocks):
        rows = pl.ds(l * tile, tile)
        local.append(
            pltpu.make_async_copy(now_ref.at[rows, here], ext[0].at[blocks + x * blocks + l], l_sem.at[2 + 2 * l])
        )
        local.append(pltpu.make_async_copy(prev_ref.at[rows, here], pv.at[x * blocks + l], l_sem.at[3 + 2 * l]))
    for c in local[2:] + local[:2]:
        c.start()

    barrier = pltpu.get_barrier_semaphore()

    def greet(j, carry):
        pl.semaphore_signal(barrier, inc=1, device_id={"rows": (me + j) % n}, device_id_type=MESH)
        return carry

    lax.fori_loop(1, n, greet, 0)
    pl.semaphore_signal(barrier, inc=1, device_id={"cols": sib}, device_id_type=MESH)
    pl.semaphore_signal(barrier, inc=1, device_id={"cols": far}, device_id_type=MESH)

    first_tile = (me - x) * blocks
    nslots = cols_ref.shape[1]
    tc = cols_ref[...]
    slot_id = lax.broadcasted_iota(jnp.int32, (blocks, nslots), 1)
    live = (slot_id < jnp.broadcast_to(count_ref[...], (blocks, nslots))) & (tc >= 0) & (tc < blocks * n)
    place = jnp.where(live, jnp.clip(tc - first_tile + blocks, 0, zero_tile - 1), zero_tile)
    vmine[...] = jnp.full(vmine.shape, zero_tile, jnp.int32)
    vmine[0:blocks, 0:nslots] = place
    for t in range(STEPS):
        ext[t][zero_tile] = jnp.zeros((tile, half), jnp.bfloat16)
    pl.semaphore_wait(barrier, n + 1)

    def start_tile(src, l):
        rows = pl.ds(l * tile, tile)
        if src == 0:
            return remote(
                now_ref.at[rows, there], ext[0].at[blocks + x * blocks + l],
                i_send.at[0, l], i_recv.at[0, l], {"rows": mate},
            )
        return remote(
            prev_ref.at[rows, there], pv.at[x * blocks + l], i_send.at[1, l], i_recv.at[1, l], {"rows": mate}
        )

    def arrived_tile(src, l):
        dst = ext[0].at[blocks + y * blocks + l] if src == 0 else pv.at[y * blocks + l]
        return remote(dst, dst, i_send.at[src, l], i_recv.at[src, l], {"rows": mate})

    places = remote(vmine, vpair, w_send.at[0], w_recv.at[me], {"rows": mate})
    places_in = remote(vmine, vpair, w_send.at[0], w_recv.at[mate], {"rows": mate})

    def tiles(k, l):
        by_far = l < 3
        src = {
            0: ham.at[l], 1: ham.at[l], 2: hb.at[1, l], 3: ham.at[l], 4: hb.at[3, l],
            5: hb.at[3, l] if by_far else hb.at[1, l], 6: hb.at[5, l],
        }[k]
        device = {
            0: {"cols": sib}, 1: {"cols": far}, 2: {"cols": sib}, 3: {"rows": mate}, 4: {"cols": sib},
            5: {"cols": far} if by_far else {"rows": mate}, 6: {"cols": sib},
        }[k]
        return remote(src, hb.at[k, l], h_send.at[k, l], h_recv.at[k, l], device)

    places.start()
    for l in range(blocks):
        start_tile(0, l).start()
    for l in range(blocks):
        tiles(3, l).start()
        tiles(1, l).start()
    for l in range(blocks):
        start_tile(1, l).start()
    for l in range(blocks):
        tiles(0, l).start()

    def halo(t, up):
        if up:
            src, dst, device = 2 * blocks, 0, me + 2
        else:
            src, dst, device = blocks, 3 * blocks, me - 2
        return remote(
            ext[t].at[pl.ds(src, blocks)], ext[t].at[pl.ds(dst, blocks)],
            t_send.at[t, int(up)], t_recv.at[t, int(up)], {"rows": device},
        )

    has_up = me + 2 < n
    has_down = me >= 2

    def send_halo(t, block):
        @pl.when((block == 0) & has_down)
        def _():
            halo(t, False).start()

        @pl.when((block == 1) & has_up)
        def _():
            halo(t, True).start()

    def recv_halo(t):
        @pl.when(has_down)
        def _():
            halo(t, True).wait_recv()

        @pl.when(has_up)
        def _():
            halo(t, False).wait_recv()

    def drain_halo(t):
        @pl.when(has_up)
        def _():
            halo(t, True).wait_send()

        @pl.when(has_down)
        def _():
            halo(t, False).wait_send()

    for c in local[2::2]:
        c.wait()
    send_halo(0, x)

    npairs = pairs.shape[0]
    natoms = sizes.shape[1]
    atom = lax.broadcasted_iota(jnp.int32, (npairs, natoms), 1)
    size_f = jnp.broadcast_to(sizes[...].astype(jnp.float32), (npairs, natoms))
    first = jnp.broadcast_to(pairs[:, 0:1], (npairs, natoms))
    second = jnp.broadcast_to(pairs[:, 1:2], (npairs, natoms))
    start = jnp.sum(jnp.where(atom < first, size_f, 0.0), axis=1, keepdims=True)
    count_a = jnp.sum(jnp.where(atom == first, size_f, 0.0), axis=1, keepdims=True)
    count_b = jnp.sum(jnp.where(atom == second, size_f, 0.0), axis=1, keepdims=True)
    all_cols = npairs * MAXF
    column = lax.broadcasted_iota(jnp.int32, (npairs, all_cols), 1)
    pair_id = lax.broadcasted_iota(jnp.int32, (npairs, all_cols), 0)
    inner = column - pair_id * MAXF
    mine = (inner >= 0) & (inner < MAXF)
    kept = mine & (inner.astype(jnp.float32) < jnp.broadcast_to(count_b, (npairs, all_cols)))

    def spread(value, where):
        return jnp.sum(
            jnp.where(where, jnp.broadcast_to(value, (npairs, all_cols)), 0.0), axis=0, keepdims=True
        )

    low = spread(start, mine)
    bounds[0] = jnp.broadcast_to(low, (8, all_cols))
    bounds[1] = jnp.broadcast_to(low + spread(count_a, kept), (8, all_cols))
    part[...] = jnp.zeros_like(part)

    for l in range(blocks):
        arrived_tile(0, l).wait_recv()
    send_halo(0, y)
    places_in.wait_recv()
    to_smem = (
        pltpu.make_async_copy(vmine, smine, l_sem.at[2 + 2 * blocks]),
        pltpu.make_async_copy(vpair, spair, l_sem.at[3 + 2 * blocks]),
    )
    for c in to_smem:
        c.start()
    for l in range(blocks):
        tiles(3, l).wait_recv()
        if l < 3:
            tiles(5, l).start()
        tiles(4, l).start()
        tiles(1, l).wait_recv()
        if l >= 3:
            tiles(5, l).start()
        tiles(2, l).start()
    for c in to_smem:
        c.wait()
    for c in local[:2] + local[3::2]:
        c.wait()

    owners = (mc, sib, far, (sib + 2) % 4)

    def row(t, l, own):
        acc = jnp.zeros((tile, half), jnp.float32)
        spots = smine if own else spair
        for q, owner in enumerate(owners):
            for s in range(own_slots):
                if own:
                    h = hown[l, s] if q == 0 else hb[q - 1, l, s]
                else:
                    h = hb[3 + q, l, s]
                v = ext[t][spots[l, owner * own_slots + s]]
                acc += jnp.dot(h, v, preferred_element_type=jnp.float32)
        at = (x if own else y) * blocks + l
        before = pv[at] if t == 0 else ext[t - 1][blocks + at]
        nxt = (2.0 * acc - before.astype(jnp.float32)).astype(jnp.bfloat16)
        if t < STEPS - 1:
            ext[t + 1][blocks + at] = nxt
        elif not own:
            fin[l] = nxt
        if own:
            rows = pl.ds(pl.multiple_of(l * tile, tile), tile)
            dens[rows, here] = dens[rows, here] + coef[t] * nxt.astype(jnp.float32)

    def back(t):
        src = ext[t + 1].at[pl.ds(blocks + y * blocks, blocks)] if t < STEPS - 1 else fin
        return remote(src, ret[t], r_send.at[t], r_recv.at[t], {"rows": mate})

    def own_rows(t):
        def body(l, carry):
            row(t, l, True)
            return carry

        lax.fori_loop(0, blocks, body, 0)
        if t < STEPS - 1:
            send_halo(t + 1, x)

    def mate_rows(t):
        def body(l, carry):
            row(t, l, False)
            return carry

        lax.fori_loop(0, blocks, body, 0)
        if t < STEPS - 1:
            send_halo(t + 1, y)
        back(t).start()

    recv_halo(0)
    for k in (0, 2):
        for l in range(blocks):
            tiles(k, l).wait_recv()
    own_rows(0)
    for l in range(blocks):
        tiles(5, l).wait_recv()
        tiles(6, l).start()
    for l in range(blocks):
        arrived_tile(1, l).wait_recv()
    for k in (4, 6):
        for l in range(blocks):
            tiles(k, l).wait_recv()
    mate_rows(0)
    for t in range(1, STEPS):
        recv_halo(t)
        mate_rows(t)
        own_rows(t)

    def gather_sums(span):
        def body(l, carry):
            rows = pl.ds(pl.multiple_of(l * tile, tile), tile)
            value = dens[rows, span]
            r = lax.broadcasted_iota(jnp.int32, (tile, half), 0) + (me * blocks + l) * tile
            r = r.astype(jnp.float32)
            keep = (r >= bounds[0, 0:1, span]) & (r < bounds[1, 0:1, span])
            sq = jnp.where(keep, value * value, 0.0)
            part[:, span] += jnp.sum(sq.reshape(tile // 8, 8, half), axis=0)
            return carry

        lax.fori_loop(0, blocks, body, 0)

    def add_back(times):
        def body(l, carry):
            rows = pl.ds(pl.multiple_of(l * tile, tile), tile)
            value = dens[rows, there]
            for t in times:
                value = value + coef[t] * ret[t][l].astype(jnp.float32)
            dens[rows, there] = value
            return carry

        lax.fori_loop(0, blocks, body, 0)

    gather_sums(here)
    for t in range(STEPS - 1):
        back(t).wait_recv()
    add_back(range(STEPS - 1))
    back(STEPS - 1).wait_recv()
    add_back((STEPS - 1,))
    gather_sums(there)

    places.wait_send()

    def share(j):
        return remote(part, wbuf.at[me], w_send.at[j], w_recv.at[n + me], {"rows": (me + j) % n})

    def landed(j):
        source = (me + j) % n
        return remote(part, wbuf.at[source], w_send.at[j], w_recv.at[n + source], {"rows": source})

    def push(j, carry):
        share(j).start()
        return carry

    lax.fori_loop(1, n, push, 0)
    for l in range(blocks):
        for k in range(7):
            tiles(k, l).wait_send()
        for src in range(2):
            start_tile(src, l).wait_send()
    for t in range(STEPS):
        drain_halo(t)
        back(t).wait_send()

    def collect(j, total):
        landed(j).wait_recv()
        return total + wbuf[(me + j) % n]

    total = lax.fori_loop(1, n, collect, part[...])
    summed = jnp.broadcast_to(jnp.sum(total, axis=0, keepdims=True), (npairs, all_cols))
    wib[...] = jnp.sum(jnp.where(mine, summed, 0.0), axis=1, keepdims=True)

    def drain(j, carry):
        share(j).wait_send()
        return carry

    lax.fori_loop(1, n, drain, 0)


def on_device(n, ham, cols, count, prev, now, dens_prev, coef, sizes, pairs):
    blocks, own_slots, tile, _ = ham.shape
    rows, width = now.shape
    half = width // 2
    npairs = pairs.shape[0]
    vmem = pl.BlockSpec(memory_space=pltpu.VMEM)
    smem = pl.BlockSpec(memory_space=pltpu.SMEM)
    free = pl.BlockSpec(memory_space=pl.ANY)
    dma = pltpu.SemaphoreType.DMA
    bf16 = jnp.bfloat16
    dens, wib = pl.pallas_call(
        functools.partial(kernel, n),
        out_shape=(
            jax.ShapeDtypeStruct((rows, width), jnp.float32),
            jax.ShapeDtypeStruct((npairs, 1), jnp.float32),
        ),
        in_specs=[free, vmem, vmem, free, free, free, smem, vmem, vmem],
        out_specs=(vmem, vmem),
        scratch_shapes=[
            pltpu.VMEM((blocks, own_slots, tile, tile), bf16),
            pltpu.VMEM((7, blocks, own_slots, tile, tile), bf16),
            pltpu.VMEM((2 * blocks, tile, half), bf16),
            pltpu.VMEM((blocks, tile, half), bf16),
            pltpu.VMEM((8, 128), jnp.int32),
            pltpu.VMEM((8, 128), jnp.int32),
            pltpu.SMEM((8, 128), jnp.int32),
            pltpu.SMEM((8, 128), jnp.int32),
            pltpu.VMEM((8, width), jnp.float32),
            pltpu.VMEM((2, 8, width), jnp.float32),
            pltpu.VMEM((n, 8, width), jnp.float32),
            dma((7, blocks)),
            dma((7, blocks)),
            dma((STEPS, 2)),
            dma((STEPS, 2)),
            dma((2, blocks)),
            dma((2, blocks)),
            dma((STEPS,)),
            dma((STEPS,)),
            dma((n,)),
            dma((2 * n,)),
            dma((4 + 2 * blocks,)),
        ]
        + [pltpu.VMEM((4 * blocks + 1, tile, half), bf16)] * STEPS
        + [pltpu.VMEM((blocks, tile, half), bf16)] * STEPS,
        compiler_params=pltpu.CompilerParams(
            collective_id=0, has_side_effects=True, vmem_limit_bytes=56 << 20
        ),
    )(ham, cols, count.reshape(-1, 1), prev, now, dens_prev, coef, sizes.reshape(1, -1), pairs)
    return dens, wib.reshape(npairs)


def solution(mesh):
    return jax.shard_map(
        functools.partial(on_device, mesh.shape["rows"]),
        mesh=mesh,
        in_specs=(
            P("rows", "cols", None, None),
            P("rows", None),
            P("rows"),
            P("rows", "cols"),
            P("rows", "cols"),
            P("rows", "cols"),
            P(),
            P(),
            P("cols", None),
        ),
        out_specs=(P("rows", "cols"), P("cols")),
        check_vma=False,
    )
```

time: 94.8 us -> 91 us (0.960)
  local copies, waits for them, and re-layouts: 6.87 us -> 4.27 us
  Pallas kernels: 86.3 us -> 84.4 us
    unnamed x20 -> x6, local copies, waits for them, and re-layouts: 6.87 us -> 3.62 us
    pallas_call x1, Pallas kernels: 86.3 us -> 84.4 us  [on_device(): pl.pallas_call(functools.partial(kernel, n), out_shape=(jax.ShapeDtypeStr...]
where the time goes in v2:
time: 91 us; the launch traced here: 90.7 us
  Pallas kernels  84.4 us (93%)
  local copies, waits for them, and re-layouts  4.27 us (5%)
  other arithmetic  1.32 us (1%)
    pallas_call x1, Pallas kernels, on_device(): pl.pallas_call(functools.partial(kernel, n), out_shape=(jax.ShapeDtypeStr...  84.4 us
    unnamed x6, local copies, waits for them, and re-layouts  3.62 us

profile of v2, /device:TPU:0, one launch (start us, length us, event | category | flops | bytes accessed | tf_op | source)
XLA Modules:
  0.0 90.7 jit_solution(11177434151195301529)
XLA Ops:
  0.6 0.0 copy-start.1
  0.6 0.6 copy-done.1
  1.3 0.0 copy-start
  1.3 0.6 copy.13.count_ref
  1.9 0.0 copy-done
  2.0 0.7 copy.14.pairs
  2.6 84.4 %shard_map.104 = (f32[1024,256]{1,0:T(8,128)}, f32[16,1]{1,0:T(8,128)}) custom-call(bf16[4,2,256,256]{3,2,1,0:T(8,128)(2,1)} %ham.1, s32[4,8]{1,0:T(4,128)} %cols_ref.1, s32[4,1]{1,0:T(4,128)} %copy.13.count_ref, bf16[1024,256]{1,0:T(8,128)(2,1)} %prev_ref.1, bf16[1024,256]{1,0:T(8,128)(2,1)} %now_ref.1, f32[1024,256]{1,0:T(8,128)} %dens_in.1, f32[3]{0:T(128)} %coef.1, ...), custom_call_target="tpu_custom_call" | custom-call | tf_op jit(solution)/shard_map/pallas_call | solution.py:384
  87.1 1.3 %reduce = f32[16]{0:T(128)} reduce(f32[16,1]{1,0:T(8,128)} %get-tuple-element.5, f32[]{:T(128)} %constant.3), dimensions={1}, to_apply=%get-tuple-element.5.reduce_sub_computation | reduce | bytes 132 | tf_op jit(solution)/shard_map/pallas_call | solution.py:384
  88.4 2.3 %copy.16 = f32[1024,256]{1,0:T(8,128)} copy(f32[1024,256]{1,0:T(8,128)} %get-tuple-element.8) | data formatting | bytes 2097152
Async XLA Ops:
  0.6 0.7 copy-start.1
  1.3 0.7 copy-start

commit v3 on v2

--- a/solution.py
+++ b/solution.py
@@ -141,49 +141,54 @@
     for l in range(blocks):
         tiles(0, l).start()
 
-    def halo(t, up):
+    def halo(t, up, l):
         if up:
             src, dst, device = 2 * blocks, 0, me + 2
         else:
             src, dst, device = blocks, 3 * blocks, me - 2
         return remote(
-            ext[t].at[pl.ds(src, blocks)], ext[t].at[pl.ds(dst, blocks)],
-            t_send.at[t, int(up)], t_recv.at[t, int(up)], {"rows": device},
+            ext[t].at[src + l], ext[t].at[dst + l],
+            t_send.at[t, int(up), l], t_recv.at[t, int(up), l], {"rows": device},
         )
 
     has_up = me + 2 < n
     has_down = me >= 2
 
-    def send_halo(t, block):
+    def send_halo(t, block, l):
         @pl.when((block == 0) & has_down)
         def _():
-            halo(t, False).start()
+            halo(t, False, l).start()
 
         @pl.when((block == 1) & has_up)
         def _():
-            halo(t, True).start()
+            halo(t, True, l).start()
 
     def recv_halo(t):
         @pl.when(has_down)
         def _():
-            halo(t, True).wait_recv()
+            for l in range(blocks):
+                halo(t, True, l).wait_recv()
 
         @pl.when(has_up)
         def _():
-            halo(t, False).wait_recv()
+            for l in range(blocks):
+                halo(t, False, l).wait_recv()
 
     def drain_halo(t):
         @pl.when(has_up)
         def _():
-            halo(t, True).wait_send()
+            for l in range(blocks):
+                halo(t, True, l).wait_send()
 
         @pl.when(has_down)
         def _():
-            halo(t, False).wait_send()
+            for l in range(blocks):
+                halo(t, False, l).wait_send()
 
     for c in local[2::2]:
         c.wait()
-    send_halo(0, x)
+    for l in range(blocks):
+        send_halo(0, x, l)
 
     npairs = pairs.shape[0]
     natoms = sizes.shape[1]
@@ -213,7 +218,7 @@
 
     for l in range(blocks):
         arrived_tile(0, l).wait_recv()
-    send_halo(0, y)
+        send_halo(0, y, l)
     places_in.wait_recv()
     to_smem = (
         pltpu.make_async_copy(vmine, smine, l_sem.at[2 + 2 * blocks]),
@@ -259,43 +264,46 @@
             rows = pl.ds(pl.multiple_of(l * tile, tile), tile)
             dens[rows, here] = dens[rows, here] + coef[t] * nxt.astype(jnp.float32)
 
-    def back(t):
-        src = ext[t + 1].at[pl.ds(blocks + y * blocks, blocks)] if t < STEPS - 1 else fin
-        return remote(src, ret[t], r_send.at[t], r_recv.at[t], {"rows": mate})
+    def back(t, l):
+        src = ext[t + 1].at[blocks + y * blocks + l] if t < STEPS - 1 else fin.at[l]
+        return remote(src, ret[t].at[l], r_send.at[t, l], r_recv.at[t, l], {"rows": mate})
 
     def own_rows(t):
         def body(l, carry):
             row(t, l, True)
+            if t < STEPS - 1:
+                send_halo(t + 1, x, l)
             return carry
 
         lax.fori_loop(0, blocks, body, 0)
+
+    def mate_row(t, l):
+        row(t, l, False)
         if t < STEPS - 1:
-            send_halo(t + 1, x)
+            send_halo(t + 1, y, l)
+        back(t, l).start()
 
     def mate_rows(t):
         def body(l, carry):
-            row(t, l, False)
+            mate_row(t, l)
             return carry
 
         lax.fori_loop(0, blocks, body, 0)
-        if t < STEPS - 1:
-            send_halo(t + 1, y)
-        back(t).start()
 
     recv_halo(0)
     for k in (0, 2):
         for l in range(blocks):
             tiles(k, l).wait_recv()
     own_rows(0)
-    for l in range(blocks):
-        tiles(5, l).wait_recv()
-        tiles(6, l).start()
-    for l in range(blocks):
-        arrived_tile(1, l).wait_recv()
-    for k in (4, 6):
-        for l in range(blocks):
-            tiles(k, l).wait_recv()
-    mate_rows(0)
+    for l in range(blocks + 1):
+        if l < blocks:
+            tiles(5, l).wait_recv()
+            tiles(6, l).start()
+        if l > 0:
+            arrived_tile(1, l - 1).wait_recv()
+            tiles(4, l - 1).wait_recv()
+            tiles(6, l - 1).wait_recv()
+            mate_row(0, l - 1)
     for t in range(1, STEPS):
         recv_halo(t)
         mate_rows(t)
@@ -327,9 +335,11 @@
 
     gather_sums(here)
     for t in range(STEPS - 1):
-        back(t).wait_recv()
+        for l in range(blocks):
+            back(t, l).wait_recv()
     add_back(range(STEPS - 1))
-    back(STEPS - 1).wait_recv()
+    for l in range(blocks):
+        back(STEPS - 1, l).wait_recv()
     add_back((STEPS - 1,))
     gather_sums(there)
 
@@ -354,7 +364,8 @@
             start_tile(src, l).wait_send()
     for t in range(STEPS):
         drain_halo(t)
-        back(t).wait_send()
+        for l in range(blocks):
+            back(t, l).wait_send()
 
     def collect(j, total):
         landed(j).wait_recv()
@@ -403,12 +414,12 @@
             pltpu.VMEM((n, 8, width), jnp.float32),
             dma((7, blocks)),
             dma((7, blocks)),
-            dma((STEPS, 2)),
-            dma((STEPS, 2)),
+            dma((STEPS, 2, blocks)),
+            dma((STEPS, 2, blocks)),
             dma((2, blocks)),
             dma((2, blocks)),
-            dma((STEPS,)),
-            dma((STEPS,)),
+            dma((STEPS, blocks)),
+            dma((STEPS, blocks)),
             dma((n,)),
             dma((2 * n,)),
             dma((4 + 2 * blocks,)),

time: 91 us -> 84.8 us (0.932)
  Pallas kernels: 84.4 us -> 78.3 us
    pallas_call x1, Pallas kernels: 84.4 us -> 78.3 us  [on_device(): pl.pallas_call(functools.partial(kernel, n), out_shape=(jax.ShapeDtypeStr...]
where the time goes in v3:
time: 84.8 us; the launch traced here: 84.6 us
  Pallas kernels  78.3 us (92%)
  local copies, waits for them, and re-layouts  4.27 us (5%)
  other arithmetic  1.32 us (2%)
    pallas_call x1, Pallas kernels, on_device(): pl.pallas_call(functools.partial(kernel, n), out_shape=(jax.ShapeDtypeStr...  78.3 us
    unnamed x6, local copies, waits for them, and re-layouts  3.62 us

profile of v3, /device:TPU:0, one launch (start us, length us, event | category | flops | bytes accessed | tf_op | source)
XLA Modules:
  0.0 84.6 jit_solution(7067822740000607761)
XLA Ops:
  0.6 0.0 copy-start.1
  0.6 0.6 copy-done.1
  1.3 0.0 copy-start
  1.3 0.6 copy.13.count_ref
  1.9 0.0 copy-done
  2.0 0.7 copy.14.pairs
  2.6 78.3 %shard_map.104 = (f32[1024,256]{1,0:T(8,128)}, f32[16,1]{1,0:T(8,128)}) custom-call(bf16[4,2,256,256]{3,2,1,0:T(8,128)(2,1)} %ham.1, s32[4,8]{1,0:T(4,128)} %cols_ref.1, s32[4,1]{1,0:T(4,128)} %copy.13.count_ref, bf16[1024,256]{1,0:T(8,128)(2,1)} %prev_ref.1, bf16[1024,256]{1,0:T(8,128)(2,1)} %now_ref.1, f32[1024,256]{1,0:T(8,128)} %dens_in.1, f32[3]{0:T(128)} %coef.1, ...), custom_call_target="tpu_custom_call" | custom-call | tf_op jit(solution)/shard_map/pallas_call | solution.py:395
  81.0 1.3 %reduce = f32[16]{0:T(128)} reduce(f32[16,1]{1,0:T(8,128)} %get-tuple-element.5, f32[]{:T(128)} %constant.3), dimensions={1}, to_apply=%get-tuple-element.5.reduce_sub_computation | reduce | bytes 132 | tf_op jit(solution)/shard_map/pallas_call | solution.py:395
  82.3 2.3 %copy.16 = f32[1024,256]{1,0:T(8,128)} copy(f32[1024,256]{1,0:T(8,128)} %get-tuple-element.8) | data formatting | bytes 2097152
Async XLA Ops:
  0.6 0.7 copy-start.1
  1.3 0.7 copy-start
